TPU v7x, 32 devices: a whole 2x2x4 slice. The times are simulated.
32 devices in a mesh: grp: 4 (over y, x), gx: 4 (over z), gy: 2 (over core).
Axes of the slice: x: 2, y: 2, z: 4, core: 2. Of those that a mesh axis runs over, the one named last changes fastest.
Arguments:
- fwd_now: float32 [3, 16, 16, 128], P(None, 'gx', 'gy'), may hold values from -6 to 6
- fwd_prev: float32 [3, 16, 16, 128], P(None, 'gx', 'gy'), may hold values from -6 to 6
- adj_now: float32 [16, 3, 16, 16, 128], P('grp', None, 'gx', 'gy'), may hold values from -6 to 6
- adj_prev: float32 [16, 3, 16, 16, 128], P('grp', None, 'gx', 'gy'), may hold values from -6 to 6
- lame_first: float32 [16, 16, 128], P('gx', 'gy'), may hold values from 0.5 to 2
- shear_mod: float32 [16, 16, 128], P('gx', 'gy'), may hold values from 0.3 to 1.2
- buoyancy: float32 [16, 16, 128], P('gx', 'gy'), may hold values from 0.5 to 1
- master_cell: int32 [1], replicated, may hold values from 0 to 32767
- master_lag: int32 [1], replicated, may hold values from 0 to 254
- master_trace: float32 [256, 3], replicated, may hold values from -96 to 96
- receiver_cell: int32 [16], P('grp'), may hold values from 0 to 32767
- receiver_lag: int32 [16], P('grp'), may hold values from 0 to 254
- receiver_trace: float32 [16, 256, 3], P('grp'), may hold values from -96 to 96
Outputs:
- adj_final: float32 [16, 3, 16, 16, 128], P('grp', None, 'gx', 'gy')
- kernels: float32 [2, 16, 16, 128], P(None, 'gx', 'gy', 'grp')
Inputs may be any that keep to these rules, and one draw needn't show every extreme that they name: `receiver_cell`: cell index in the whole grid, numbered (x * 16 + y) * 128 + z. `master_cell`: cell index in the whole grid, numbered (x * 16 + y) * 128 + z.
All inputs are finite; a program needn't handle non-finite values.
Results may differ from a plain program's by a relative error of at most 0.00011.
Values sent between devices are 32-bit elements; how exact they have to be, the bound alone decides.
A program may use at most 64 MiB of HBM per device.

v0:
```python
import functools

import jax
import jax.numpy as jnp
from jax import lax
from jax.experimental import pallas as pl
from jax.experimental.pallas import tpu as pltpu
from jax.sharding import PartitionSpec as P

STEPS = 2
MESH = pl.DeviceIdType.MESH

time_step_sq = 0.0625


def kernel(
    sizes,
    master_cell,
    master_lag,
    master_trace,
    receiver_cell,
    receiver_lag,
    receiver_trace,
    fwd_now,
    fwd_prev,
    adj_now,
    adj_prev,
    lame_first,
    shear_mod,
    buoyancy,
    adj_out,
    kern_out,
    now,
    prev,
    mid,
    lame,
    shear,
    buoy,
    xlo,
    xhi,
    ylo,
    yhi,
    row_first,
    row_last,
    mod_send,
    mod_recv,
    low_stress,
    totals,
    share_send,
    share_recv,
    cells,
    amps,
    master_trace_s,
    receiver_cell_s,
    receiver_lag_s,
    receiver_trace_s,
    load_sem,
    send_sem,
    recv_sem,
):
    groups, count_x, count_y = sizes
    receivers, _, cells_x, cells_y, depth = adj_now.shape
    fields = receivers + 1
    grp = lax.axis_index("grp")
    gx = lax.axis_index("gx")
    gy = lax.axis_index("gy")
    has_down = gx > 0
    has_up = gx < count_x - 1
    has_left = gy > 0
    has_right = gy < count_y - 1
    corner_ul = jnp.logical_and(has_up, has_left)
    corner_dr = jnp.logical_and(has_down, has_right)
    down = (grp, gx - 1, gy)
    up = (grp, gx + 1, gy)
    left = (grp, gx, gy - 1)
    right = (grp, gx, gy + 1)
    up_left = (grp, gx + 1, gy - 1)
    down_right = (grp, gx - 1, gy + 1)
    peers = [(lax.rem(grp + d, groups), gx, gy) for d in range(1, groups)]
    sides = (
        (has_down, down),
        (has_up, up),
        (has_left, left),
        (has_right, right),
        (corner_ul, up_left),
        (corner_dr, down_right),
    )

    loads = [
        (adj_now, now.at[pl.ds(0, receivers)]),
        (fwd_now, now.at[receivers]),
        (lame_first, lame.at[pl.ds(1, cells_x)]),
        (shear_mod, shear.at[pl.ds(1, cells_x)]),
        (adj_prev, prev.at[pl.ds(0, receivers)]),
        (fwd_prev, prev.at[receivers]),
        (buoyancy, buoy),
        (master_trace, master_trace_s),
        (receiver_cell, receiver_cell_s),
        (receiver_lag, receiver_lag_s),
        (receiver_trace, receiver_trace_s),
    ]
    loads = [pltpu.make_async_copy(src, dst, load_sem.at[i]) for i, (src, dst) in enumerate(loads)]
    for copy in loads:
        copy.start()

    barrier = pltpu.get_barrier_semaphore()
    expected = jnp.int32(groups - 1)
    for there, where in sides:
        expected = expected + there.astype(jnp.int32)

        @pl.when(there)
        def _():
            pl.semaphore_signal(barrier, inc=1, device_id=where, device_id_type=MESH)

    for where in peers:
        pl.semaphore_signal(barrier, inc=1, device_id=where, device_id_type=MESH)

    @pl.when(jnp.logical_not(has_down))
    def _():
        xlo[...] = jnp.zeros_like(xlo)
        lame[0] = jnp.zeros_like(lame[0])
        shear[0] = jnp.zeros_like(shear[0])

    @pl.when(jnp.logical_not(has_up))
    def _():
        xhi[...] = jnp.zeros_like(xhi)

    @pl.when(jnp.logical_not(has_left))
    def _():
        ylo[:, :, 0:cells_x] = jnp.zeros_like(ylo[:, :, 0:cells_x])
        mod_recv[...] = jnp.zeros_like(mod_recv)

    @pl.when(jnp.logical_not(has_right))
    def _():
        yhi[:, :, 1 : cells_x + 1] = jnp.zeros_like(yhi[:, :, 1 : cells_x + 1])

    @pl.when(jnp.logical_not(corner_ul))
    def _():
        ylo[:, :, cells_x] = jnp.zeros_like(ylo[:, :, cells_x])

    @pl.when(jnp.logical_not(corner_dr))
    def _():
        yhi[:, :, 0] = jnp.zeros_like(yhi[:, :, 0])

    row_first[...] = jnp.zeros_like(row_first)
    row_last[...] = jnp.zeros_like(row_last)

    pl.semaphore_wait(barrier, expected)

    number = [0]

    def remote(src, dst, where):
        i = number[0]
        number[0] += 1
        return pltpu.make_async_remote_copy(
            src_ref=src,
            dst_ref=dst,
            send_sem=send_sem.at[i],
            recv_sem=recv_sem.at[i],
            device_id=where,
            device_id_type=MESH,
        )

    def rows(k):
        return [
            (remote(row_first.at[k, :, cells_x - 1], yhi.at[k, :, 0], up_left), corner_ul, corner_dr),
            (remote(row_last.at[k, :, 0], ylo.at[k, :, cells_x], down_right), corner_dr, corner_ul),
            (remote(row_first.at[k], yhi.at[k, :, pl.ds(1, cells_x)], left), has_left, has_right),
            (remote(row_last.at[k], ylo.at[k, :, pl.ds(0, cells_x)], right), has_right, has_left),
        ]

    def start(copies):
        for copy, sends, _ in copies:
            pl.when(sends)(copy.start)

    def arrive(copies):
        for copy, _, gets in copies:
            pl.when(gets)(copy.wait_recv)

    def sent(copies):
        for copy, sends, _ in copies:
            pl.when(sends)(copy.wait_send)

    last = cells_x - 1
    split = (receivers + 2) // 2
    group = pl.ds(0, split)
    rest = pl.ds(split, receivers - split)
    rest_all = pl.ds(split, fields - split)
    first_x = [
        (remote(adj_now.at[group, :, 0], xhi.at[0, group], down), has_down, has_up),
        (remote(adj_now.at[group, :, last], xlo.at[0, group], up), has_up, has_down),
    ]
    first_moduli = [
        (remote(lame_first.at[last], lame.at[0], up), has_up, has_down),
        (remote(shear_mod.at[last], shear.at[0], up), has_up, has_down),
        (remote(mod_send, mod_recv, right), has_right, has_left),
    ]
    first_rest = [
        (remote(adj_now.at[rest, :, 0], xhi.at[0, rest], down), has_down, has_up),
        (remote(adj_now.at[rest, :, last], xlo.at[0, rest], up), has_up, has_down),
        (remote(fwd_now.at[:, 0], xhi.at[0, receivers], down), has_down, has_up),
        (remote(fwd_now.at[:, last], xlo.at[0, receivers], up), has_up, has_down),
    ]
    first_rows = rows(0)
    start(first_moduli[:2])
    start(first_x)
    start(first_rest)

    for copy in loads[:4]:
        copy.wait()

    for f in range(fields):
        for c in range(3):
            for x in range(cells_x):
                row_first[0, c, x, f : f + 1, :] = now[f, c, x, 0:1, :]
                row_last[0, c, x, f : f + 1, :] = now[f, c, x, cells_y - 1 : cells_y, :]
    for x in range(cells_x):
        mod_send[x : x + 1] = lame[x + 1, cells_y - 1 : cells_y, :]
        mod_send[cells_x + x : cells_x + x + 1] = shear[x + 1, cells_y - 1 : cells_y, :]

    start(first_rows)
    start(first_moduli[2:])

    for copy in loads[4:]:
        copy.wait()

    for f in range(fields):
        master = f == receivers
        cells[f] = master_cell[0] if master else receiver_cell_s[f]
        lag = master_lag[0] if master else receiver_lag_s[f]
        for k in range(STEPS):
            for c in range(3):
                spot = (f * STEPS + k) * 3 + c
                amps[spot] = master_trace_s[c, lag + k] if master else receiver_trace_s[c, f, lag + k]

    row_at = lax.broadcasted_iota(jnp.int32, (cells_y, depth), 0)
    lane_at = lax.broadcasted_iota(jnp.int32, (cells_y, depth), 1)
    flat_at = row_at * depth + lane_at
    top = row_at == 0
    bottom = row_at == cells_y - 1
    front = lane_at == 0
    back = lane_at == depth - 1
    plane_cells = cells_y * count_y * depth
    first_cell = gx * cells_x * plane_cells + gy * cells_y * depth

    def next_z(v):
        return jnp.where(back, 0.0, pltpu.roll(v, depth - 1, 1))

    def last_z(v):
        return jnp.where(front, 0.0, pltpu.roll(v, 1, 1))

    def next_y(v, row):
        return jnp.where(bottom, row, pltpu.roll(v, cells_y - 1, 0))

    def last_y(v, row):
        return jnp.where(top, row, pltpu.roll(v, 1, 0))

    def wall(k):
        for x in range(cells_x):
            here = [ylo[k, c, x] for c in range(3)]
            beside = [ylo[k, c, x + 1] for c in range(3)]
            above = [row_first[k, c, x] for c in range(3)]
            lam = mod_recv[x : x + 1]
            mu = mod_recv[cells_x + x : cells_x + x + 1]
            grad_y = [above[c] - here[c] for c in range(3)]
            xy = grad_y[0] + (beside[1] - here[1])
            yz = (next_z(here[1]) - here[1]) + grad_y[2]
            dilation = (beside[0] - here[0]) + grad_y[1] + (next_z(here[2]) - here[2])
            low_stress[k, 0, x] = mu * xy
            low_stress[k, 1, x] = lam * dilation + 2.0 * mu * grad_y[1]
            low_stress[k, 2, x] = mu * yz

    def step(k, f, state, earlier, put):
        one = slice(f, f + 1)

        def row(c, x):
            return yhi[k, c, x + 1, one, :]

        here = [xlo[k, f, c] for c in range(3)]
        lam = lame[0]
        mu = shear[0]
        after = [state[f, c, 0] for c in range(3)]
        across = [next_y(here[c], row(c, -1)) for c in range(2)]
        along = [next_z(here[c]) for c in (0, 2)]
        xx = after[0] - here[0]
        dilation = xx + (across[1] - here[1]) + (along[1] - here[2])
        low = [
            lam * dilation + 2.0 * mu * xx,
            mu * ((across[0] - here[0]) + (after[1] - here[1])),
            mu * ((along[0] - here[0]) + (after[2] - here[2])),
        ]
        cell = cells[f]
        amp = [amps[(f * STEPS + k) * 3 + c] for c in range(3)]
        for x in range(cells_x):
            here = after
            after = [state[f, c, x + 1] if x < last else xhi[k, f, c] for c in range(3)]
            lam = lame[x + 1]
            mu = shear[x + 1]
            twice = 2.0 * mu
            gx_ = [after[c] - here[c] for c in range(3)]
            gy_ = [next_y(here[c], row(c, x)) - here[c] for c in range(3)]
            gz_ = [next_z(here[c]) - here[c] for c in range(3)]
            spread = lam * (gx_[0] + gy_[1] + gz_[2])
            xx = spread + twice * gx_[0]
            yy = spread + twice * gy_[1]
            zz = spread + twice * gz_[2]
            xy = mu * (gy_[0] + gx_[1])
            xz = mu * (gz_[0] + gx_[2])
            yz = mu * (gz_[1] + gy_[2])
            wall_xy, wall_yy, wall_yz = [low_stress[k, j, x, one, :] for j in range(3)]
            force = [
                (xx - low[0]) + (xy - last_y(xy, wall_xy)) + (xz - last_z(xz)),
                (xy - low[1]) + (yy - last_y(yy, wall_yy)) + (yz - last_z(yz)),
                (xz - low[2]) + (yz - last_y(yz, wall_yz)) + (zz - last_z(zz)),
            ]
            low = [xx, xy, xz]
            placed = flat_at == cell - (first_cell + x * plane_cells)
            scaled = time_step_sq * buoy[x]
            for c in range(3):
                moved = force[c] + jnp.where(placed, amp[c], 0.0)
                put(f, c, x, 2.0 * here[c] - earlier[f, c, x] + scaled * moved)

    def strain(planes, rows):
        for x in range(cells_x):
            here, after = planes[x], planes[x + 1]
            gx_ = [after[c] - here[c] for c in range(3)]
            gy_ = [next_y(here[c], rows[x][c]) - here[c] for c in range(3)]
            gz_ = [next_z(here[c]) - here[c] for c in range(3)]
            yield (
                gx_[0],
                gy_[1],
                gz_[2],
                gy_[0] + gx_[1],
                gz_[0] + gx_[2],
                gz_[1] + gy_[2],
            )

    def correlate(k, state):
        def summed(load):
            total = load(0)
            for f in range(1, receivers):
                total = total + load(f)
            return total

        whole, master = [], []
        for x in range(cells_x + 1):
            if x < cells_x:
                whole.append([summed(lambda f: state[f, c, x]) for c in range(3)])
                master.append([state[receivers, c, x] for c in range(3)])
            else:
                whole.append([summed(lambda f: xhi[k, f, c]) for c in range(3)])
                master.append([xhi[k, receivers, c] for c in range(3)])
        whole_rows = [
            [summed(lambda f: yhi[k, c, x + 1, f : f + 1, :]) for c in range(3)]
            for x in range(cells_x)
        ]
        master_rows = [
            [yhi[k, c, x + 1, receivers : receivers + 1, :] for c in range(3)]
            for x in range(cells_x)
        ]
        pairs = zip(strain(whole, whole_rows), strain(master, master_rows))
        for x, (a, b) in enumerate(pairs):
            swell = (a[0] + a[1] + a[2]) * (b[0] + b[1] + b[2])
            twist = 2.0 * (a[0] * b[0] + a[1] * b[1] + a[2] * b[2])
            twist = twist + (a[3] * b[3] + a[4] * b[4] + a[5] * b[5])
            if k == 0:
                totals[0, x] = swell
                totals[1, x] = twist
            else:
                totals[0, x] += swell
                totals[1, x] += twist

    arrive(first_moduli)
    arrive(first_rows)
    wall(0)
    arrive(first_x)

    def put_mid(f, c, x, value):
        mid[f, c, x] = value
        row_first[1, c, x, f : f + 1, :] = value[0:1]
        row_last[1, c, x, f : f + 1, :] = value[cells_y - 1 : cells_y]

    for f in range(split):
        step(0, f, now, prev, put_mid)
    second_x = [
        (remote(mid.at[group, :, 0], xhi.at[1, group], down), has_down, has_up),
        (remote(mid.at[group, :, last], xlo.at[1, group], up), has_up, has_down),
    ]
    start(second_x)
    arrive(first_rest)
    for f in range(split, fields):
        step(0, f, now, prev, put_mid)
    second_rest = [
        (remote(mid.at[rest_all, :, 0], xhi.at[1, rest_all], down), has_down, has_up),
        (remote(mid.at[rest_all, :, last], xlo.at[1, rest_all], up), has_up, has_down),
    ]
    second_rows = rows(1)
    start(second_rest)
    start(second_rows)
    second_round = second_x + second_rest + second_rows
    correlate(0, now)
    arrive(second_round)
    correlate(1, mid)

    share = depth // groups
    lane_part = lane_at // share
    for g in range(groups):
        for j in range(2):
            packed = None
            for x in range(cells_x):
                turn = (share * (x - g)) % depth
                piece = totals[j, x] if turn == 0 else pltpu.roll(totals[j, x], turn, 1)
                packed = piece if packed is None else jnp.where(lane_part == x, piece, packed)
            share_send[g, j] = packed
    third_round = [
        (remote(share_send.at[peers[d][0]], share_recv.at[d], peers[d]), True, True)
        for d in range(groups - 1)
    ]
    for copy, _, _ in third_round:
        copy.start()

    def put_out(f, c, x, value):
        adj_out[f, c, x] = value

    wall(1)
    for f in range(receivers):
        step(1, f, mid, now, put_out)

    for copy, _, _ in third_round:
        copy.wait_recv()
    scale_out = 1.0 / (STEPS * receivers * groups)
    for j in range(2):
        part = share_send[grp, j]
        for d in range(groups - 1):
            part = part + share_recv[d, j]
        part = part * scale_out
        for x in range(cells_x):
            piece = part if x == 0 else pltpu.roll(part, depth - share * x, 1)
            kern_out[j, x] = piece[:, 0:share]
    sent(first_x + first_moduli + first_rest + first_rows)
    sent(second_round)
    for copy, _, _ in third_round:
        copy.wait_send()


def local(
    fwd_now,
    fwd_prev,
    adj_now,
    adj_prev,
    lame_first,
    shear_mod,
    buoyancy,
    master_cell,
    master_lag,
    master_trace,
    receiver_cell,
    receiver_lag,
    receiver_trace,
):
    cells_x, cells_y, depth = lame_first.shape
    receivers = adj_now.shape[0]
    fields = receivers + 1
    sizes = tuple(lax.axis_size(axis) for axis in ("grp", "gx", "gy"))
    groups = sizes[0]
    lanes = -(-fields // 8) * 8
    block = (fields, 3, cells_x, cells_y, depth)
    scalar = pl.BlockSpec(memory_space=pltpu.SMEM)
    whole = pl.BlockSpec(memory_space=pltpu.HBM)
    vector = pl.BlockSpec(memory_space=pltpu.VMEM)

    def room(*shape):
        return pltpu.VMEM(shape, jnp.float32)

    def stay(value):
        return pltpu.with_memory_space_constraint(value, pltpu.HBM)

    return pl.pallas_call(
        functools.partial(kernel, sizes),
        out_shape=(
            pltpu.VMEM(adj_now.shape, jnp.float32),
            pltpu.VMEM((2, cells_x, cells_y, depth // groups), jnp.float32),
        ),
        in_specs=[scalar] * 2 + [whole] * 11,
        out_specs=(vector, vector),
        scratch_shapes=[
            room(*block),
            room(*block),
            room(*block),
            room(cells_x + 1, cells_y, depth),
            room(cells_x + 1, cells_y, depth),
            room(cells_x, cells_y, depth),
            room(STEPS, fields, 3, cells_y, depth),
            room(STEPS, fields, 3, cells_y, depth),
            room(STEPS, 3, cells_x + 1, lanes, depth),
            room(STEPS, 3, cells_x + 1, lanes, depth),
            room(STEPS, 3, cells_x, lanes, depth),
            room(STEPS, 3, cells_x, lanes, depth),
            room(2 * cells_x, depth),
            room(2 * cells_x, depth),
            room(STEPS, 3, cells_x, lanes, depth),
            room(2, cells_x, cells_y, depth),
            room(groups, 2, cells_y, depth),
            room(groups - 1, 2, cells_y, depth),
            pltpu.SMEM((fields,), jnp.int32),
            pltpu.SMEM((fields * STEPS * 3,), jnp.float32),
            pltpu.SMEM((3,) + master_trace.shape[:1], jnp.float32),
            pltpu.SMEM((receivers,), jnp.int32),
            pltpu.SMEM((receivers,), jnp.int32),
            pltpu.SMEM((3,) + receiver_trace.shape[:2], jnp.float32),
            pltpu.SemaphoreType.DMA((11,)),
            pltpu.SemaphoreType.DMA((32,)),
            pltpu.SemaphoreType.DMA((32,)),
        ],
        compiler_params=pltpu.CompilerParams(
            collective_id=0, has_side_effects=True, vmem_limit_bytes=32 * 1024 * 1024
        ),
    )(
        master_cell,
        master_lag,
        stay(master_trace.T),
        stay(receiver_cell),
        stay(receiver_lag),
        stay(receiver_trace.transpose(2, 0, 1)),
        stay(fwd_now),
        stay(fwd_prev),
        stay(adj_now),
        stay(adj_prev),
        stay(lame_first),
        stay(shear_mod),
        stay(buoyancy),
    )


def solution(mesh):
    in_specs = (
        P(None, "gx", "gy", None),
        P(None, "gx", "gy", None),
        P("grp", None, "gx", "gy", None),
        P("grp", None, "gx", "gy", None),
        P("gx", "gy", None),
        P("gx", "gy", None),
        P("gx", "gy", None),
        P(),
        P(),
        P(),
        P("grp"),
        P("grp"),
        P("grp", None, None),
    )
    out_specs = (P("grp", None, "gx", "gy", None), P(None, "gx", "gy", "grp"))
    return jax.shard_map(local, mesh=mesh, in_specs=in_specs, out_specs=out_specs, check_vma=False)
```

profile of v0, /device:TPU:0, one launch (start us, length us, event | category | flops | bytes accessed | tf_op | source)
XLA Modules:
  0.0 19.6 jit_solution(8260616059477074534)
XLA Ops:
  1.9 16.4 %shard_map.140 = (f32[4,3,4,8,128]{4,3,2,1,0:T(8,128)S(1)}, f32[2,4,8,32]{3,2,1,0:T(8,128)S(1)}) custom-call(s32[1]{0:T(128)S(6)} %copy.19.master_cell, s32[1]{0:T(128)S(6)} %copy.20.master_lag, f32[3,256]{1,0:T(4,128)} %bitcast.3, s32[4]{0:T(128)} %receiver_cell.1, s32[4]{0:T(128)} %receiver_lag.1, f32[3,4,256]{2,1,0:T(4,128)} %bitcast.2, ...), custom_call_target="tpu_custom_call" | custom-call | tf_op jit(solution)/shard_map/pallas_call | solution.py:478
  18.3 0.7 %copy.17 = f32[4,3,4,8,128]{4,3,2,1,0:T(8,128)} copy(f32[4,3,4,8,128]{4,3,2,1,0:T(8,128)S(1)} %get-tuple-element.2) | data formatting | bytes 393216
  19.0 0.6 %copy.18 = f32[2,4,8,32]{3,2,1,0:T(8,128)} copy(f32[2,4,8,32]{3,2,1,0:T(8,128)S(1)} %get-tuple-element.3) | data formatting | bytes 16384
where the time goes:
time: 19.8 us; the launch traced here: 19.6 us
  Pallas kernels  16.4 us (83%)
  between operations  1.93 us (10%)
  local copies, waits for them, and re-layouts  1.29 us (7%)
    pallas_call x1, Pallas kernels, local(): pl.pallas_call(functools.partial(kernel, sizes), out_shape=(pltpu.VMEM(ad...  16.4 us
    unnamed x2, local copies, waits for them, and re-layouts  1.29 us

commit v1 on v0

--- a/solution.py
+++ b/solution.py
@@ -378,7 +378,7 @@
     def put_mid(f, c, x, value):
         mid[f, c, x] = value
         row_first[1, c, x, f : f + 1, :] = value[0:1]
-        row_last[1, c, x, f : f + 1, :] = value[cells_y - 1 : cells_y]
+        row_last[1, c, x, f : f + 1, :] = mid[f, c, x, cells_y - 1 : cells_y, :]
 
     for f in range(split):
         step(0, f, now, prev, put_mid)
@@ -441,6 +441,15 @@
     sent(second_round)
     for copy, _, _ in third_round:
         copy.wait_send()
+
+
+def hand_over(adj_made, kern_made, adj_out, kern_out, sems):
+    adj_copy = pltpu.make_async_copy(adj_made, adj_out, sems.at[0])
+    kern_copy = pltpu.make_async_copy(kern_made, kern_out, sems.at[1])
+    adj_copy.start()
+    kern_copy.start()
+    adj_copy.wait()
+    kern_copy.wait()
 
 
 def local(
@@ -475,7 +484,7 @@
     def stay(value):
         return pltpu.with_memory_space_constraint(value, pltpu.HBM)
 
-    return pl.pallas_call(
+    made = pl.pallas_call(
         functools.partial(kernel, sizes),
         out_shape=(
             pltpu.VMEM(adj_now.shape, jnp.float32),
@@ -530,6 +539,14 @@
         stay(shear_mod),
         stay(buoyancy),
     )
+    made = [pltpu.with_memory_space_constraint(value, pltpu.VMEM) for value in made]
+    return pl.pallas_call(
+        hand_over,
+        out_shape=tuple(jax.ShapeDtypeStruct(value.shape, value.dtype) for value in made),
+        in_specs=[pl.BlockSpec(memory_space=pltpu.VMEM)] * 2,
+        out_specs=(whole, whole),
+        scratch_shapes=[pltpu.SemaphoreType.DMA((2,))],
+    )(*made)
 
 
 def solution(mesh):

time: 19.8 us -> 19.2 us (0.970)
  local copies, waits for them, and re-layouts: 1.29 us -> 0 us
  Pallas kernels: 16.4 us -> 17.1 us
    unnamed x2 -> x0, local copies, waits for them, and re-layouts: 1.29 us -> none
    pallas_call x0 -> x1, Pallas kernels: none -> 0.7 us  [local(): pl.pallas_call(hand_over, out_shape=tuple((jax.ShapeDtypeStruct(value.sha...]
where the time goes in v1:
time: 19.2 us; the launch traced here: 19 us
  Pallas kernels  17.1 us (89%)
  between operations  1.93 us (10%)
    pallas_call x1, Pallas kernels, local(): pl.pallas_call(functools.partial(kernel, sizes), out_shape=(pltpu.VMEM(ad...  16.4 us
    pallas_call x1, Pallas kernels, local(): pl.pallas_call(hand_over, out_shape=tuple((jax.ShapeDtypeStruct(value.sha...  0.7 us

profile of v1, /device:TPU:0, one launch (start us, length us, event | category | flops | bytes accessed | tf_op | source)
XLA Modules:
  0.0 19.0 jit_solution(2607750134009300353)
XLA Ops:
  1.9 16.4 %shard_map.140 = (f32[4,3,4,8,128]{4,3,2,1,0:T(8,128)S(1)}, f32[2,4,8,32]{3,2,1,0:T(8,128)S(1)}) custom-call(s32[1]{0:T(128)S(6)} %copy.15.master_cell, s32[1]{0:T(128)S(6)} %copy.16.master_lag, f32[3,256]{1,0:T(4,128)} %bitcast.3, s32[4]{0:T(128)} %receiver_cell.1, s32[4]{0:T(128)} %receiver_lag.1, f32[3,4,256]{2,1,0:T(4,128)} %bitcast.2, ...), custom_call_target="tpu_custom_call" | custom-call | tf_op jit(solution)/shard_map/pallas_call | solution.py:487
  18.3 0.7 %shard_map.141 = (f32[4,3,4,8,128]{4,3,2,1,0:T(8,128)}, f32[2,4,8,32]{3,2,1,0:T(8,128)}) custom-call(f32[4,3,4,8,128]{4,3,2,1,0:T(8,128)S(1)} %get-tuple-element.4.adj_made, f32[2,4,8,32]{3,2,1,0:T(8,128)S(1)} %get-tuple-element.5.kern_made), custom_call_target="tpu_custom_call" | custom-call | tf_op jit(solution)/shard_map/pallas_call | solution.py:543

commit v2 on v1

--- a/solution.py
+++ b/solution.py
@@ -86,6 +86,18 @@
         (corner_dr, down_right),
     )
 
+    barrier = pltpu.get_barrier_semaphore()
+    expected = jnp.int32(groups - 1)
+    for there, where in sides:
+        expected = expected + there.astype(jnp.int32)
+
+        @pl.when(there)
+        def _():
+            pl.semaphore_signal(barrier, inc=1, device_id=where, device_id_type=MESH)
+
+    for where in peers:
+        pl.semaphore_signal(barrier, inc=1, device_id=where, device_id_type=MESH)
+
     loads = [
         (adj_now, now.at[pl.ds(0, receivers)]),
         (fwd_now, now.at[receivers]),
@@ -103,48 +115,6 @@
     for copy in loads:
         copy.start()
 
-    barrier = pltpu.get_barrier_semaphore()
-    expected = jnp.int32(groups - 1)
-    for there, where in sides:
-        expected = expected + there.astype(jnp.int32)
-
-        @pl.when(there)
-        def _():
-            pl.semaphore_signal(barrier, inc=1, device_id=where, device_id_type=MESH)
-
-    for where in peers:
-        pl.semaphore_signal(barrier, inc=1, device_id=where, device_id_type=MESH)
-
-    @pl.when(jnp.logical_not(has_down))
-    def _():
-        xlo[...] = jnp.zeros_like(xlo)
-        lame[0] = jnp.zeros_like(lame[0])
-        shear[0] = jnp.zeros_like(shear[0])
-
-    @pl.when(jnp.logical_not(has_up))
-    def _():
-        xhi[...] = jnp.zeros_like(xhi)
-
-    @pl.when(jnp.logical_not(has_left))
-    def _():
-        ylo[:, :, 0:cells_x] = jnp.zeros_like(ylo[:, :, 0:cells_x])
-        mod_recv[...] = jnp.zeros_like(mod_recv)
-
-    @pl.when(jnp.logical_not(has_right))
-    def _():
-        yhi[:, :, 1 : cells_x + 1] = jnp.zeros_like(yhi[:, :, 1 : cells_x + 1])
-
-    @pl.when(jnp.logical_not(corner_ul))
-    def _():
-        ylo[:, :, cells_x] = jnp.zeros_like(ylo[:, :, cells_x])
-
-    @pl.when(jnp.logical_not(corner_dr))
-    def _():
-        yhi[:, :, 0] = jnp.zeros_like(yhi[:, :, 0])
-
-    row_first[...] = jnp.zeros_like(row_first)
-    row_last[...] = jnp.zeros_like(row_last)
-
     pl.semaphore_wait(barrier, expected)
 
     number = [0]
@@ -205,6 +175,36 @@
     start(first_moduli[:2])
     start(first_x)
     start(first_rest)
+
+    @pl.when(jnp.logical_not(has_down))
+    def _():
+        xlo[...] = jnp.zeros_like(xlo)
+        lame[0] = jnp.zeros_like(lame[0])
+        shear[0] = jnp.zeros_like(shear[0])
+
+    @pl.when(jnp.logical_not(has_up))
+    def _():
+        xhi[...] = jnp.zeros_like(xhi)
+
+    @pl.when(jnp.logical_not(has_left))
+    def _():
+        ylo[:, :, 0:cells_x] = jnp.zeros_like(ylo[:, :, 0:cells_x])
+        mod_recv[...] = jnp.zeros_like(mod_recv)
+
+    @pl.when(jnp.logical_not(has_right))
+    def _():
+        yhi[:, :, 1 : cells_x + 1] = jnp.zeros_like(yhi[:, :, 1 : cells_x + 1])
+
+    @pl.when(jnp.logical_not(corner_ul))
+    def _():
+        ylo[:, :, cells_x] = jnp.zeros_like(ylo[:, :, cells_x])
+
+    @pl.when(jnp.logical_not(corner_dr))
+    def _():
+        yhi[:, :, 0] = jnp.zeros_like(yhi[:, :, 0])
+
+    row_first[...] = jnp.zeros_like(row_first)
+    row_last[...] = jnp.zeros_like(row_last)
 
     for copy in loads[:4]:
         copy.wait()
@@ -395,11 +395,15 @@
         (remote(mid.at[rest_all, :, last], xlo.at[1, rest_all], up), has_up, has_down),
     ]
     second_rows = rows(1)
-    start(second_rest)
-    start(second_rows)
+    start(second_rest[:1])
+    start(second_rows[:3:2])
+    start(second_rest[1:])
+    start(second_rows[1::2])
     second_round = second_x + second_rest + second_rows
+    uppers = [second_x[0], second_rest[0], second_rows[2]]
+    others = [second_x[1], second_rest[1], second_rows[0], second_rows[1], second_rows[3]]
     correlate(0, now)
-    arrive(second_round)
+    arrive(uppers)
     correlate(1, mid)
 
     share = depth // groups
@@ -422,6 +426,7 @@
     def put_out(f, c, x, value):
         adj_out[f, c, x] = value
 
+    arrive(others)
     wall(1)
     for f in range(receivers):
         step(1, f, mid, now, put_out)

time: 19.2 us -> 19.2 us (level)
  no operation moved by 1% of the time
where the time goes in v2:
time: 19.2 us; the launch traced here: 19 us
  Pallas kernels  17.1 us (89%)
  between operations  1.93 us (10%)
    pallas_call x1, Pallas kernels, local(): pl.pallas_call(functools.partial(kernel, sizes), out_shape=(pltpu.VMEM(ad...  16.4 us
    pallas_call x1, Pallas kernels, local(): pl.pallas_call(hand_over, out_shape=tuple((jax.ShapeDtypeStruct(value.sha...  0.7 us

profile of v2, /device:TPU:0, one launch (start us, length us, event | category | flops | bytes accessed | tf_op | source)
XLA Modules:
  0.0 19.0 jit_solution(8221468672991001342)
XLA Ops:
  1.9 16.4 %shard_map.140 = (f32[4,3,4,8,128]{4,3,2,1,0:T(8,128)S(1)}, f32[2,4,8,32]{3,2,1,0:T(8,128)S(1)}) custom-call(s32[1]{0:T(128)S(6)} %copy.15.master_cell, s32[1]{0:T(128)S(6)} %copy.16.master_lag, f32[3,256]{1,0:T(4,128)} %bitcast.3, s32[4]{0:T(128)} %receiver_cell.1, s32[4]{0:T(128)} %receiver_lag.1, f32[3,4,256]{2,1,0:T(4,128)} %bitcast.2, ...), custom_call_target="tpu_custom_call" | custom-call | tf_op jit(solution)/shard_map/pallas_call | solution.py:492
  18.3 0.7 %shard_map.141 = (f32[4,3,4,8,128]{4,3,2,1,0:T(8,128)}, f32[2,4,8,32]{3,2,1,0:T(8,128)}) custom-call(f32[4,3,4,8,128]{4,3,2,1,0:T(8,128)S(1)} %get-tuple-element.4.adj_made, f32[2,4,8,32]{3,2,1,0:T(8,128)S(1)} %get-tuple-element.5.kern_made), custom_call_target="tpu_custom_call" | custom-call | tf_op jit(solution)/shard_map/pallas_call | solution.py:548
